TPU v7x, 32 devices: a whole 2x2x4 slice. The times are simulated.
32 devices in a mesh: groups: 2 (over x), train: 16 (over z, y, core).
Axes of the slice: x: 2, y: 2, z: 4, core: 2. Of those that a mesh axis runs over, the one named last changes fastest.
Arguments:
- query_grads: bfloat16 [768, 8192], P(('groups', 'train')), parts along dimension 0
- train_grads: bfloat16 [8192, 8192], P(('groups', 'train')), parts along dimension 0
- precondition: float32 [16384], P('groups'), parts along dimension 0, may hold values from 0.2 to 5
- routes: int32 [768, 4], P('groups'), parts along dimension 0, may hold values from 0 to 15, all different within a row; in each aligned block of 24 rows (0 to 23, 24 to 47, ...) at most 8 rows name the same one
- owner: int32 [32], P('groups'), parts along dimension 0, may hold values from 0 to 15, each once
- counts: int32 [32], P(('groups', 'train')), parts along dimension 0, may hold values from 32 to 256, as said below
Outputs:
- scores: float32 [768, 4, 256], P(('groups', 'train')), parts along dimension 0
There are 2 independent parts, one for each index of `groups`. A program takes and returns all parts, laid end to end along the dimension named above; each array names one. Nothing has to cross between parts.
Inputs may be any that keep to these rules, and one draw needn't show every extreme that they name: `routes`: each row names 4 different train shards; among the 24 queries of one block no shard is named by more than 8, and in some blocks a shard is named by exactly 8; every shard is named by some query. `owner`: A permutation of the train devices. `counts`: some shard is full and some holds exactly 32 examples; the valid examples are the first ones of a shard.
All inputs are finite; a program needn't handle non-finite values.
Results may differ from a plain program's by a relative error of at most 0.003.
Values may be sent and summed in bfloat16 or wider, within the bound.
A program may use at most 128 MiB of HBM per device.

v0:
```python
import math

import jax
import jax.numpy as jnp
from jax import lax
from jax.sharding import PartitionSpec as P

CAP = 8


def normalize(query_grads, precondition):
    scaled = query_grads.astype(jnp.float32) * precondition[None, :]
    spread = jnp.sqrt(jnp.mean(scaled * scaled, axis=1, keepdims=True) + 1e-06)
    return (scaled / spread).astype(jnp.bfloat16)


def slot_table(block_routes, shards):
    hit_table = jnp.sum(
        (block_routes[:, :, None] == jnp.arange(shards, dtype=jnp.int32)[None, None, :]).astype(
            jnp.int32
        ),
        axis=1,
        dtype=jnp.int32,
    )
    earlier = jnp.cumsum(hit_table, axis=0, dtype=jnp.int32) - hit_table
    return jnp.take_along_axis(earlier, block_routes, axis=1)


def fetch_home(result):
    return lax.all_to_all(result, "train", split_axis=0, concat_axis=0, tiled=True)


def per_device(query_grads, train_grads, precondition, routes, owner, counts):
    shards = lax.axis_size("train")
    position = lax.axis_index("train")
    block_size = query_grads.shape[0]
    features = train_grads.shape[1]
    capacity = CAP
    normed = normalize(query_grads, precondition)
    own_routes = lax.dynamic_slice_in_dim(routes, position * block_size, block_size, 0)
    target = own_routes * capacity + slot_table(own_routes, shards)
    lane_ids = jnp.arange(shards * capacity, dtype=jnp.int32)
    picked = jnp.any(target[:, :, None] == lane_ids[None, None, :], axis=1).astype(jnp.bfloat16)
    outgoing = lax.dot_general(
        picked, normed, (((0,), (0,)), ((), ())), preferred_element_type=jnp.float32
    )
    outgoing = outgoing.astype(jnp.bfloat16).reshape(shards, capacity, features)
    inverse = jnp.zeros((shards,), jnp.int32).at[owner].set(jnp.arange(shards, dtype=jnp.int32))
    row_norm = jnp.sqrt(jnp.mean(jnp.square(train_grads.astype(jnp.float32)), axis=1) + 1e-06)
    filled = jnp.arange(train_grads.shape[0], dtype=jnp.int32) < counts[0]
    arrived = lax.all_to_all(outgoing, "train", split_axis=0, concat_axis=0, tiled=True)
    flattened = arrived.reshape(-1, features)
    dotted = lax.dot_general(
        flattened, train_grads, (((1,), (1,)), ((), ())), preferred_element_type=jnp.float32
    )
    result = jnp.where(filled[None, :], dotted / (row_norm[None, :] * math.sqrt(features)), 0.0)
    result = result.reshape(arrived.shape[0], arrived.shape[1], -1)
    returned = fetch_home(result[inverse])
    owned_block = inverse[position]
    their_routes = lax.dynamic_slice_in_dim(routes, owned_block * block_size, block_size, 0)
    pickup = their_routes * capacity + slot_table(their_routes, shards)
    return returned.reshape(shards * capacity, -1)[pickup]


def solution(mesh):
    return jax.shard_map(
        per_device,
        mesh=mesh,
        in_specs=(
            P(("groups", "train"), None),
            P(("groups", "train"), None),
            P("groups"),
            P("groups", None),
            P("groups"),
            P(("groups", "train")),
        ),
        out_specs=P(("groups", "train"), None, None),
        check_vma=False,
    )
```

profile of v0, /device:TPU:0, one launch (start us, length us, event | category | flops | bytes accessed | tf_op | source)
XLA Modules:
  0.0 82.8 jit_solution(15365235174695581197)
XLA Ops:
  0.0 0.7 compare_select_fusion.4
  0.7 0.6 scatter_custom_fusion
  1.3 0.6 dynamic_slice.10
  2.5 1.2 %multiply_reduce_fusion.1 = f32[24]{0:T(128)S(1)} fusion(bf16[24,8192]{1,0:T(8,128)(2,1)} %param.8, f32[8192]{0:T(1024)} %param.10), kind=kLoop, calls=%fused_computation.14 | loop fusion | flops 786408 | bytes 426080 | tf_op jit(solution)/shard_map/reduce_sum | solution.py:13
  3.8 0.8 constant_dynamic-slice_fusion
  4.5 0.1 copy.32
  4.6 0.1 copy.23
  4.7 0.1 copy.24
  4.8 0.1 reshape.101
  5.0 0.1 copy.21
  5.1 0.0 copy-start
  5.1 0.0 copy-start.1
  5.1 1.3 %gather_fusion.2 = s32[96]{0:T(128)S(1)} fusion(s32[24,16]{1,0:T(8,128)S(1)} %sub.6, s32[96]{0:T(128)S(1)} %reshape.101), kind=kCustom, calls=%fused_computation.clone | custom fusion | bytes 1536 | tf_op jit(solution)/shard_map/jit(take_along_axis)/gather | solution.py:26
  6.4 0.1 reshape.104
  6.5 0.1 copy.25
  6.6 0.1 fusion.14
  6.7 0.0 copy-done
  6.7 0.0 copy-done.1
  6.7 2.1 %fusion = bf16[16,8,8192]{2,1,0:T(8,128)(2,1)} fusion(pred[24,128]{1,0:T(8,128)(4,1)S(1)} %fusion.14, bf16[24,8192]{1,0:T(8,128)(2,1)S(1)} %copy-done, f32[24]{0:T(128)S(1)} %add_sqrt_fusion, f32[8192]{0:T(1024)S(1)} %copy-done.1), kind=kOutput, calls=%fused_computation.6 | convolution fusion | flops 52166656 | bytes 2526304 | tf_op jit(solution)/shard_map/dot_general | solution.py:44
  8.8 7.4 %all-to-all-start = ((bf16[16,8,8192]{2,1,0:T(8,128)(2,1)}), bf16[16,8,8192]{2,1,0:T(8,128)(2,1)S(1)}, u32[]{:S(2)}, u32[]{:S(2)}) async-start(bf16[16,8,8192]{2,1,0:T(8,128)(2,1)} %fusion), calls=%async_computation | async-start | bytes 4194304 | tf_op jit(solution)/shard_map/all_to_all | solution.py:51
  16.3 0.1 copy.33
  17.0 0.1 copy.30
  17.1 0.1 copy.31
  17.2 0.1 reshape.106
  17.3 0.1 copy.28
  17.4 1.3 %gather_fusion.3 = s32[96]{0:T(128)S(1)} fusion(s32[24,16]{1,0:T(8,128)S(1)} %sub.7, s32[96]{0:T(128)S(1)} %reshape.106), kind=kCustom, calls=%fused_computation.1.clone | custom fusion | bytes 1536 | tf_op jit(solution)/shard_map/jit(take_along_axis)/gather | solution.py:26
  18.7 0.1 reshape.109
  18.8 3.1 %multiply_reduce_fusion = f32[256]{0:T(256)S(1)} fusion(bf16[256,8192]{1,0:T(8,128)(2,1)} %param.9), kind=kLoop, calls=%fused_computation.7 | loop fusion | flops 6291200 | bytes 4195328 | tf_op jit(solution)/shard_map/reduce_sum | solution.py:49
  22.0 35.4 %all-to-all-done = bf16[16,8,8192]{2,1,0:T(8,128)(2,1)S(1)} async-done(((bf16[16,8,8192]{2,1,0:T(8,128)(2,1)}), bf16[16,8,8192]{2,1,0:T(8,128)(2,1)S(1)}, u32[]{:S(2)}, u32[]{:S(2)}) %all-to-all-start) | async-done | bytes 2097184 | tf_op jit(solution)/shard_map/all_to_all | solution.py:51
  57.4 3.7 %fusion.9 = f32[16,8,256]{2,1,0:T(8,128)S(1)} fusion(bf16[256,8192]{1,0:T(8,128)(2,1)} %param.9, bf16[16,8,8192]{2,1,0:T(8,128)(2,1)S(1)} %all-to-all-done, f32[256]{0:T(256)S(1)} %sqrt_multiply_fusion, pred[256]{0:T(512)(128)(4,1)S(1)} %iota_compare_fusion.3), kind=kOutput, calls=%fused_computation.12 | convolution fusion | flops 536936448 | bytes 6423808 | tf_op jit(solution)/shard_map/dot_general | solution.py:53
  61.1 1.2 %gather_fusion = f32[16,8,256]{2,1,0:T(8,128)} fusion(f32[16,8,256]{2,1,0:T(8,128)S(1)} %fusion.9, s32[1024]{0:T(1024)S(1)} %pad_clamp_fusion.1), kind=kCustom, calls=%fused_computation.2 | custom fusion | bytes 262208 | tf_op jit(solution)/shard_map/gather | solution.py:58
  62.3 11.2 %all-to-all-start.1 = ((f32[16,8,256]{2,1,0:T(8,128)}), f32[16,8,256]{2,1,0:T(8,128)S(1)}, u32[]{:S(2)}, u32[]{:S(2)}) async-start(f32[16,8,256]{2,1,0:T(8,128)} %gather_fusion), calls=%async_computation.1 | async-start | bytes 262144 | tf_op jit(solution)/shard_map/all_to_all | solution.py:30
  73.5 0.1 reshape.72
  73.6 7.8 %all-to-all-done.1 = f32[16,8,256]{2,1,0:T(8,128)S(1)} async-done(((f32[16,8,256]{2,1,0:T(8,128)}), f32[16,8,256]{2,1,0:T(8,128)S(1)}, u32[]{:S(2)}, u32[]{:S(2)}) %all-to-all-start.1) | async-done | bytes 131104 | tf_op jit(solution)/shard_map/all_to_all | solution.py:30
  81.5 0.7 gather_fusion.1
  82.2 0.7 reshape.71
  (18 shorter events, 0.2 us)
Async XLA Ops:
  5.1 1.6 %copy-start = (bf16[24,8192]{1,0:T(8,128)(2,1)S(1)}, bf16[24,8192]{1,0:T(8,128)(2,1)}, u32[]{:S(2)}) copy-start(bf16[24,8192]{1,0:T(8,128)(2,1)} %param.8) | copy-start | bytes 1179652
  5.1 1.6 %copy-start.1 = (f32[8192]{0:T(1024)S(1)}, f32[8192]{0:T(1024)}, u32[]{:S(2)}) copy-start(f32[8192]{0:T(1024)} %param.10) | copy-start | bytes 98308
  8.8 48.6 %all-to-all-start = ((bf16[16,8,8192]{2,1,0:T(8,128)(2,1)}), bf16[16,8,8192]{2,1,0:T(8,128)(2,1)S(1)}, u32[]{:S(2)}, u32[]{:S(2)}) async-start(bf16[16,8,8192]{2,1,0:T(8,128)(2,1)} %fusion), calls=%async_computation | async-start | bytes 4194304 | tf_op jit(solution)/shard_map/all_to_all | solution.py:51
  62.3 19.2 %all-to-all-start.1 = ((f32[16,8,256]{2,1,0:T(8,128)}), f32[16,8,256]{2,1,0:T(8,128)S(1)}, u32[]{:S(2)}, u32[]{:S(2)}) async-start(f32[16,8,256]{2,1,0:T(8,128)} %gather_fusion), calls=%async_computation.1 | async-start | bytes 262144 | tf_op jit(solution)/shard_map/all_to_all | solution.py:30
where the time goes:
time: 83.2 us; the launch traced here: 82.8 us
  waiting for transfers between devices  43.2 us (52%)
  starting transfers between devices  18.7 us (22%)
  local copies, waits for them, and re-layouts  8.32 us (10%)
  matrix products  5.85 us (7%)
  other arithmetic  5.28 us (6%)
  between operations  1.5 us (2%)
    all_to_all x1, waiting for transfers between devices, per_device(): lax.all_to_all(outgoing, 'train', split_axis=0, concat_axis=0, tiled=True)  35.4 us
    all_to_all x1, starting transfers between devices, fetch_home(): lax.all_to_all(result, 'train', split_axis=0, concat_axis=0, tiled=True)  11.2 us
    all_to_all x1, waiting for transfers between devices, fetch_home(): lax.all_to_all(result, 'train', split_axis=0, concat_axis=0, tiled=True)  7.81 us
    all_to_all x1, starting transfers between devices, per_device(): lax.all_to_all(outgoing, 'train', split_axis=0, concat_axis=0, tiled=True)  7.44 us
    dot_general x1, matrix products, per_device(): lax.dot_general(flattened, train_grads, (((1,), (1,)), ((), ())), preferr...  3.72 us
    gather x10, local copies, waits for them, and re-layouts, slot_table(): return jnp.take_along_axis(earlier, block_routes, axis=1)  3.25 us
    reduce_sum x1, other arithmetic, per_device(): jnp.mean(jnp.square(train_grads.astype(jnp.float32)), axis=1) + 1e-06  3.1 us
    dot_general x1, matrix products, per_device(): lax.dot_general(picked, normed, (((0,), (0,)), ((), ())), preferred_eleme...  2.13 us
  transfers between devices with their start and end apart: 2, of which 2 were waited for; matrix products, arithmetic and copies ran while one was open for 6% of the time, Pallas kernels for 0%

commit v1 on v0

--- a/solution.py
+++ b/solution.py
@@ -3,6 +3,8 @@
 import jax
 import jax.numpy as jnp
 from jax import lax
+from jax.experimental import pallas as pl
+from jax.experimental.pallas import tpu as pltpu
 from jax.sharding import PartitionSpec as P
 
 CAP = 8
@@ -62,9 +64,326 @@
     return returned.reshape(shards * capacity, -1)[pickup]
 
 
+LINE = 4
+PARTS = 4
+
+
+def grid_kernel(routes_pairs, routes_flat, owner, counts, query, scale, train, out,
+                other, held, train_vmem, scaled, picked, select, results, outgoing, incoming,
+                raw_sem, train_sem, z_send, z_recv, y_send, y_recv, c_send, c_recv, s_send, s_recv):
+    rows, features = query.shape
+    pair = 2 * rows
+    total = held.shape[2]
+    extra = total - pair
+    width = held.shape[3]
+    columns = train_vmem.shape[0]
+    shards = 4 * LINE
+    me = lax.axis_index("train")
+    core = me % 2
+    side = (me // 2) % 2
+    place = me // 4
+    mate = place * 4 + side * 2 + (1 - core)
+    across = place * 4 + (1 - side) * 2 + core
+    after, before = me + 4, me - 4
+
+    barrier = pltpu.get_barrier_semaphore()
+    for hop in range(1, shards):
+        pl.semaphore_signal(barrier, inc=1, device_id={"train": (me + hop) % shards},
+                            device_id_type=pl.DeviceIdType.MESH)
+    load = pltpu.make_async_copy(train, train_vmem, train_sem)
+    load.start()
+
+    def remote(source, target, send, recv, device):
+        return pltpu.make_async_remote_copy(
+            src_ref=source, dst_ref=target, send_sem=send, recv_sem=recv,
+            device_id={"train": device}, device_id_type=pl.DeviceIdType.MESH)
+
+    def z_copy(direction, step, origin, part, device):
+        block = held.at[origin, core * PARTS + part, pl.ds(0, pair)]
+        return remote(block, block, z_send.at[direction, step, part], z_recv.at[origin, part], device)
+
+    def y_copy(origin, part):
+        block = held.at[origin, core * PARTS + part, pl.ds(pair, extra)]
+        return remote(picked.at[origin, part], block, y_send.at[origin, part], y_recv.at[origin, part], across)
+
+    def c_copy(kind, origin, part, lane):
+        span = pl.ds(0, pair) if kind == 0 else pl.ds(pair, extra)
+        block = held.at[origin, lane * PARTS + part, span]
+        return remote(block, block, c_send.at[kind, origin, part], c_recv.at[kind, origin, part], mate)
+
+    def slots(pairs, shard):
+        hit = jnp.sum((pairs == shard).astype(jnp.float32), axis=0, keepdims=True)
+        first = lax.broadcasted_iota(jnp.int32, (pair, pair), 0)
+        second = lax.broadcasted_iota(jnp.int32, (pair, pair), 1)
+        earlier = ((first // rows == second // rows) & (first < second)).astype(jnp.float32)
+        order = jnp.dot(jnp.broadcast_to(hit, (8, pair)), earlier, preferred_element_type=jnp.float32)[:1]
+        return hit, order.astype(jnp.int32)
+
+    def spread(block):
+        def body(i, total_square):
+            at = pl.ds(pl.multiple_of(i * width, width), width)
+            value = block[:, at].astype(jnp.float32) * scale[:, at]
+            return total_square + jnp.sum(value * value, axis=1, keepdims=True)
+        square = lax.fori_loop(0, features // width, body, jnp.zeros((rows, 1), jnp.float32))
+        return jnp.sqrt(square / features + 1e-06)
+
+    for origin in range(LINE):
+        pairs = routes_pairs[origin * 2 + side]
+        tables = []
+        for core_there in range(2):
+            hit, order = slots(pairs, place * 4 + (1 - side) * 2 + core_there)
+            tables.append((hit, order))
+        line = lax.broadcasted_iota(jnp.int32, (extra, pair), 0)
+        lane = lax.broadcasted_iota(jnp.int32, (extra, pair), 1)
+        second_core = (line // CAP) % 2 == 1
+        hit = jnp.where(second_core, tables[1][0], tables[0][0])
+        order = jnp.where(second_core, tables[1][1], tables[0][1])
+        chosen = (hit > 0.5) & (order == line % CAP) & (line // (2 * CAP) == lane // rows)
+        select[origin] = chosen.astype(jnp.float32).astype(jnp.bfloat16)
+
+    my_spread = spread(query)
+    pl.semaphore_wait(barrier, shards - 1)
+    swap = remote(query, other, raw_sem.at[0], raw_sem.at[1], mate)
+    swap.start()
+    swap.wait_recv()
+    their_spread = spread(other)
+    spread_first = jnp.where(core == 0, my_spread, their_spread)
+    spread_second = jnp.where(core == 0, their_spread, my_spread)
+
+    def cross(origin, part):
+        block = held[origin, core * PARTS + part, pl.ds(0, pair), :]
+        chosen = jnp.dot(select[origin], block, preferred_element_type=jnp.float32)
+        picked[origin, part] = chosen.astype(jnp.bfloat16)
+        y_copy(origin, part).start()
+
+    def first(part, carry):
+        at = pl.ds(pl.multiple_of((core * PARTS + part) * width, width), width)
+        mine = query[:, at].astype(jnp.float32) * scale[:, at]
+        theirs = other[:, at].astype(jnp.float32) * scale[:, at]
+        top = jnp.where(core == 0, mine, theirs) / spread_first
+        low = jnp.where(core == 0, theirs, mine) / spread_second
+        held[place, core * PARTS + part, pl.ds(0, pair), :] = jnp.concatenate([top, low], axis=0).astype(jnp.bfloat16)
+
+        @pl.when(place < LINE - 1)
+        def _():
+            z_copy(0, 0, place, part, after).start()
+
+        @pl.when(place > 0)
+        def _():
+            z_copy(1, 0, place, part, before).start()
+
+        c_copy(0, place, part, core).start()
+        cross(place, part)
+        return carry
+
+    lax.fori_loop(0, PARTS, first, 0)
+
+    def sources(step):
+        if step == 0:
+            return [(None, place, None)]
+        return [(place >= step, place - step, 0), (place + step < LINE, place + step, 1)]
+
+    def under(condition, body):
+        if condition is None:
+            body()
+        else:
+            pl.when(condition)(body)
+
+    def arrive(step, part):
+        for condition, origin, direction in sources(step):
+            def body(origin=origin, direction=direction):
+                z_copy(direction, 0, origin, part, mate).wait_recv()
+                if step < LINE - 1:
+                    if direction == 0:
+                        @pl.when(place < LINE - 1)
+                        def _():
+                            z_copy(0, step, origin, part, after).start()
+                    else:
+                        @pl.when(place > 0)
+                        def _():
+                            z_copy(1, step, origin, part, before).start()
+                c_copy(0, origin, part, core).start()
+                cross(origin, part)
+            under(condition, body)
+
+    def crossed(step, part):
+        for condition, origin, _ in sources(step):
+            def body(origin=origin):
+                y_copy(origin, part).wait_recv()
+                c_copy(1, origin, part, core).start()
+            under(condition, body)
+
+    def multiply(step, part):
+        for condition, origin, _ in sources(step):
+            def body(origin=origin):
+                c_copy(0, origin, part, 1 - core).wait_recv()
+                c_copy(1, origin, part, 1 - core).wait_recv()
+                partial = jnp.zeros((total, columns), jnp.float32)
+                for lane in range(2):
+                    at = pl.ds(pl.multiple_of((lane * PARTS + part) * width, width), width)
+                    partial = partial + lax.dot_general(
+                        held[origin, lane * PARTS + part], train_vmem[:, at], (((1,), (1,)), ((), ())),
+                        preferred_element_type=jnp.float32)
+                results[origin] += partial
+            under(condition, body)
+
+    def loop(*work):
+        def body(part, carry):
+            for call, step in work:
+                call(step, part)
+            return carry
+        lax.fori_loop(0, PARTS, body, 0)
+
+    results[...] = jnp.zeros_like(results)
+    load.wait()
+
+    def square(i, sums):
+        at = pl.ds(pl.multiple_of(i * 128, 128), 128)
+        value = train_vmem[:, at].astype(jnp.float32)
+        return sums + value * value
+
+    sums = lax.fori_loop(0, features // 128, square, jnp.zeros((columns, 128), jnp.float32))
+    sums = jnp.sum(jnp.transpose(sums), axis=0, keepdims=True)
+    norm = jnp.sqrt(sums / features + 1e-06) * math.sqrt(features)
+    live = lax.broadcasted_iota(jnp.int32, (1, columns), 1) < counts[0]
+    scaled[...] = norm
+
+    loop((arrive, 1), (crossed, 0))
+    loop((multiply, 0))
+    loop((arrive, 2), (crossed, 1))
+    loop((multiply, 1))
+
+    flat = jnp.zeros((1, routes_flat.shape[1]), jnp.int32)
+    for block in range(shards):
+        flat = flat + jnp.where(owner[block] == me, routes_flat[block:block + 1, :], 0)
+    lanes = flat.shape[1]
+    fan = routes_pairs.shape[1]
+    wide = jnp.broadcast_to(flat.astype(jnp.float32), (lanes, lanes))
+    same = jnp.transpose(wide) == wide
+    first_lane = lax.broadcasted_iota(jnp.int32, (lanes, lanes), 0) // fan
+    second_lane = lax.broadcasted_iota(jnp.int32, (lanes, lanes), 1) // fan
+    order = jnp.sum((same & (first_lane < second_lane)).astype(jnp.int32), axis=0, keepdims=True)
+    goal = flat * CAP + order
+    pickup = (lax.broadcasted_iota(jnp.int32, (shards * CAP, lanes), 0) == goal).astype(jnp.float32)
+    pickup = jnp.transpose(pickup)
+
+    loop((arrive, 3), (crossed, 2))
+    loop((multiply, 2))
+    loop((crossed, 3), (multiply, 3))
+
+    gathered = jnp.zeros((shards * CAP, columns), jnp.float32)
+    for origin in range(LINE):
+        hit, order = slots(routes_pairs[origin * 2 + side], me)
+        line = lax.broadcasted_iota(jnp.int32, (shards * CAP, pair), 0)
+        lane = lax.broadcasted_iota(jnp.int32, (shards * CAP, pair), 1)
+        near = (origin * 2 + side) * 2
+        home = jnp.where(lane < rows, owner[near], owner[near + 1])
+        chosen = ((hit > 0.5) & (order == line % CAP) & (home == line // CAP)).astype(jnp.float32)
+        gathered = gathered + jnp.dot(chosen, results[origin, :pair], precision=lax.Precision.HIGHEST,
+                                      preferred_element_type=jnp.float32)
+        line = lax.broadcasted_iota(jnp.int32, (shards * CAP, extra), 0)
+        lane = lax.broadcasted_iota(jnp.int32, (shards * CAP, extra), 1)
+        far = (origin * 2 + 1 - side) * 2
+        home = jnp.where(lane < 2 * CAP, owner[far], owner[far + 1])
+        chosen = ((lane // CAP) % 2 == core) & (lane % CAP == line % CAP) & (home == line // CAP)
+        gathered = gathered + jnp.dot(chosen.astype(jnp.float32), results[origin, pair:],
+                                      precision=lax.Precision.HIGHEST, preferred_element_type=jnp.float32)
+    gathered = jnp.where(live, gathered / scaled[...], 0.0)
+    outgoing[...] = gathered.reshape(shards, CAP, columns)
+    incoming[me] = outgoing[me]
+
+    def score_copy(hop, peer):
+        return remote(outgoing.at[peer], incoming.at[me], s_send.at[hop], s_recv.at[hop], peer)
+
+    def send(hop, carry):
+        score_copy(hop, (me + hop) % shards).start()
+        return carry
+
+    lax.fori_loop(1, shards, send, 0)
+
+    def receive(hop, carry):
+        source = (me + shards - hop) % shards
+        remote(outgoing.at[source], incoming.at[source], s_send.at[hop], s_recv.at[hop], source).wait_recv()
+        return carry
+
+    lax.fori_loop(1, shards, receive, 0)
+    out[...] = jnp.dot(pickup, incoming[...].reshape(shards * CAP, columns),
+                       precision=lax.Precision.HIGHEST, preferred_element_type=jnp.float32)
+
+    swap.wait_send()
+
+    def finish(part, carry):
+        for origin in range(LINE):
+            y_copy(origin, part).wait_send()
+            for kind in range(2):
+                c_copy(kind, origin, part, core).wait_send()
+        for step in range(LINE - 1):
+            @pl.when((place >= step) & (place < LINE - 1))
+            def _():
+                z_copy(0, step, place - step, part, after).wait_send()
+
+            @pl.when((place + step < LINE) & (place > 0))
+            def _():
+                z_copy(1, step, place + step, part, before).wait_send()
+        return carry
+
+    lax.fori_loop(0, PARTS, finish, 0)
+
+    def sent(hop, carry):
+        score_copy(hop, (me + hop) % shards).wait_send()
+        return carry
+
+    lax.fori_loop(1, shards, sent, 0)
+
+
+def on_grid(query_grads, train_grads, precondition, routes, owner, counts):
+    rows, features = query_grads.shape
+    columns = train_grads.shape[0]
+    fan = routes.shape[1]
+    shards = 4 * LINE
+    pair, extra = 2 * rows, 4 * CAP
+    width = features // (2 * PARTS)
+    routes_pairs = jnp.transpose(routes.reshape(2 * LINE, pair, fan), (0, 2, 1))
+    routes_flat = routes.reshape(shards, rows * fan)
+    vmem = pl.BlockSpec(memory_space=pltpu.VMEM)
+    smem = pl.BlockSpec(memory_space=pltpu.SMEM)
+    dma = pltpu.SemaphoreType.DMA
+    out = pl.pallas_call(
+        grid_kernel,
+        out_shape=jax.ShapeDtypeStruct((rows * fan, columns), jnp.float32),
+        in_specs=[vmem, vmem, smem, smem, vmem, vmem, pl.BlockSpec(memory_space=pl.ANY)],
+        out_specs=vmem,
+        scratch_shapes=[
+            pltpu.VMEM((rows, features), jnp.bfloat16),
+            pltpu.VMEM((LINE, 2 * PARTS, pair + extra, width), jnp.bfloat16),
+            pltpu.VMEM((columns, features), jnp.bfloat16),
+            pltpu.VMEM((1, columns), jnp.float32),
+            pltpu.VMEM((LINE, PARTS, extra, width), jnp.bfloat16),
+            pltpu.VMEM((LINE, extra, pair), jnp.bfloat16),
+            pltpu.VMEM((LINE, pair + extra, columns), jnp.float32),
+            pltpu.VMEM((shards, CAP, columns), jnp.float32),
+            pltpu.VMEM((shards, CAP, columns), jnp.float32),
+            dma((2,)),
+            dma,
+            dma((2, LINE - 1, PARTS)),
+            dma((LINE, PARTS)),
+            dma((LINE, PARTS)),
+            dma((LINE, PARTS)),
+            dma((2, LINE, PARTS)),
+            dma((2, LINE, PARTS)),
+            dma((shards,)),
+            dma((shards,)),
+        ],
+        compiler_params=pltpu.CompilerParams(
+            collective_id=0, has_side_effects=True, vmem_limit_bytes=40 * 1024 * 1024),
+    )(routes_pairs, routes_flat, owner, counts, query_grads, precondition.reshape(1, features), train_grads)
+    return out.reshape(rows, fan, columns)
+
+
 def solution(mesh):
+    per_part = on_grid if mesh.shape["train"] == 4 * LINE else per_device
     return jax.shard_map(
-        per_device,
+        per_part,
         mesh=mesh,
         in_specs=(
             P(("groups", "train"), None),

time: 83.2 us -> 58.9 us (0.71)
  Pallas kernels: 0 us -> 50.9 us
  waiting for transfers between devices: 43.2 us -> 0 us
  starting transfers between devices: 18.7 us -> 0 us
  matrix products: 5.85 us -> 0 us
  other arithmetic: 5.28 us -> 0 us
  local copies, waits for them, and re-layouts: 8.32 us -> 6.97 us
    pallas_call x0 -> x1, Pallas kernels: none -> 50.9 us  [on_grid(): pl.pallas_call(grid_kernel, out_shape=jax.ShapeDtypeStruct((rows * fan, c...]
    all_to_all x2 -> x0, waiting for transfers between devices: 43.2 us -> none  [the longest x1 35.4 us: per_device(): lax.all_to_all(outgoing, 'train', split_axis=0, concat_axis=0, tiled=True)]
    all_to_all x2 -> x0, starting transfers between devices: 18.7 us -> none  [the longest x1 11.2 us: fetch_home(): lax.all_to_all(result, 'train', split_axis=0, concat_axis=0, tiled=True)]
    dot_general x2 -> x0, matrix products: 5.85 us -> none  [the longest x1 3.72 us: per_device(): lax.dot_general(flattened, train_grads, (((1,), (1,)), ((), ())), preferr...]
    gather x13 -> x0, local copies, waits for them, and re-layouts: 5.82 us -> none  [the longest x10 3.25 us: slot_table(): return jnp.take_along_axis(earlier, block_routes, axis=1)]
    unnamed x6 -> x9, local copies, waits for them, and re-layouts: 0.18 us -> 5.41 us
    reduce_sum x3 -> x0, other arithmetic: 4.33 us -> none  [the longest x1 3.1 us: per_device(): jnp.mean(jnp.square(train_grads.astype(jnp.float32)), axis=1) + 1e-06]
    reshape x0 -> x4, local copies, waits for them, and re-layouts: none -> 1.56 us  [the longest x2 0.78 us: on_grid(): routes_pairs = jnp.transpose(routes.reshape(2 * LINE, pair, fan), (0, 2, 1))]
  transfers between devices with their start and end apart: 2 -> 0, of which waited for: 2 -> 0; matrix products, arithmetic and copies ran while one was open for 6% -> 0% of each run, Pallas kernels for 0% -> 0%
where the time goes in v1:
time: 58.9 us; the launch traced here: 58.6 us
  Pallas kernels  50.9 us (86%)
  local copies, waits for them, and re-layouts  6.97 us (12%)
  between operations  0.69 us (1%)
    pallas_call x1, Pallas kernels, on_grid(): pl.pallas_call(grid_kernel, out_shape=jax.ShapeDtypeStruct((rows * fan, c...  50.9 us
    unnamed x9, local copies, waits for them, and re-layouts  5.41 us

profile of v1, /device:TPU:0, one launch (start us, length us, event | category | flops | bytes accessed | tf_op | source)
XLA Modules:
  0.0 58.6 jit_solution(13637192510593692284)
XLA Ops:
  0.0 0.8 %copy.9 = s32[384,4]{1,0:T(8,128)S(1)} copy(s32[384,4]{0,1:T(4,128)} %param.9) | data formatting | bytes 12288 | tf_op args[3]
  0.8 0.1 reshape.13.routes_flat
  0.9 0.8 %reshape.12 = s32[8,48,4]{1,0,2:T(8,128)S(1)} reshape(s32[384,4]{0,1:T(4,128)} %param.9) | data formatting | bytes 12288 | tf_op jit(solution)/shard_map/reshape | solution.py:346
  2.4 0.0 copy-start
  2.4 2.2 %copy-done = bf16[256,8192]{1,0:T(8,128)(2,1)S(1)} copy-done((bf16[256,8192]{1,0:T(8,128)(2,1)S(1)}, bf16[256,8192]{1,0:T(8,128)(2,1)}, u32[]{:S(2)}) %copy-start) | copy-done | bytes 4194328
  4.6 0.0 copy-start.1
  4.6 1.0 %copy-done.1 = bf16[24,8192]{1,0:T(8,128)(2,1)S(1)} copy-done((bf16[24,8192]{1,0:T(8,128)(2,1)S(1)}, bf16[24,8192]{1,0:T(8,128)(2,1)}, u32[]{:S(2)}) %copy-start.1) | copy-done | bytes 393240
  5.6 0.0 copy-start.2
  5.6 0.8 %copy-done.2 = f32[8192]{0:T(1024)S(1)} copy-done((f32[8192]{0:T(1024)S(1)}, f32[8192]{0:T(1024)}, u32[]{:S(2)}) %copy-start.2) | copy-done | bytes 32792
  6.3 0.0 copy-start.3
  6.3 0.7 %copy-done.3 = s32[16]{0:T(128)S(1)} copy-done((s32[16]{0:T(128)S(1)}, s32[16]{0:T(128)}, u32[]{:S(2)}) %copy-start.3) | copy-done | bytes 88
  7.0 50.9 %shard_map.64 = f32[96,256]{1,0:T(8,128)S(1)} custom-call(s32[8,4,48]{2,1,0:T(4,128)S(1)} %bitcast.6, s32[16,96]{1,0:T(8,128)S(1)} %reshape.13.routes_flat, s32[16]{0:T(128)S(1)} %copy-done.3, s32[1]{0:T(128)S(6)} %copy.12.counts, bf16[24,8192]{1,0:T(8,128)(2,1)S(1)} %copy-done.1, f32[1,8192]{1,0:T(1,128)S(1)} %bitcast.7, bf16[256,8192]{1,0:T(8,128)(2,1)S(1)} %copy-done), custom_call_target="tpu_custom_call" | custom-call | tf_op jit(solution)/shard_map/pallas_call | solution.py:351
  57.9 0.7 %reshape.15 = f32[24,4,256]{2,1,0:T(4,128)} reshape(f32[96,256]{1,0:T(8,128)S(1)} %shard_map.64) | data formatting | bytes 196608 | tf_op jit(solution)/shard_map/reshape | solution.py:380
  (1 shorter events, 0.0 us)
Async XLA Ops:
  2.4 2.2 %copy-start = (bf16[256,8192]{1,0:T(8,128)(2,1)S(1)}, bf16[256,8192]{1,0:T(8,128)(2,1)}, u32[]{:S(2)}) copy-start(bf16[256,8192]{1,0:T(8,128)(2,1)} %train.1) | copy-start | bytes 12582916
  4.6 1.0 %copy-start.1 = (bf16[24,8192]{1,0:T(8,128)(2,1)S(1)}, bf16[24,8192]{1,0:T(8,128)(2,1)}, u32[]{:S(2)}) copy-start(bf16[24,8192]{1,0:T(8,128)(2,1)} %query.1) | copy-start | bytes 1179652
  5.6 0.8 %copy-start.2 = (f32[8192]{0:T(1024)S(1)}, f32[8192]{0:T(1024)}, u32[]{:S(2)}) copy-start(f32[8192]{0:T(1024)} %param.8) | copy-start | bytes 98308
  6.3 0.7 %copy-start.3 = (s32[16]{0:T(128)S(1)}, s32[16]{0:T(128)}, u32[]{:S(2)}) copy-start(s32[16]{0:T(128)} %owner.1) | copy-start | bytes 196

commit v2 on v1

--- a/solution.py
+++ b/solution.py
@@ -68,10 +68,14 @@
 PARTS = 4
 
 
-def grid_kernel(routes_pairs, routes_flat, owner, counts, query, scale, train, out,
-                other, held, train_vmem, scaled, picked, select, results, outgoing, incoming,
-                raw_sem, train_sem, z_send, z_recv, y_send, y_recv, c_send, c_recv, s_send, s_recv):
+def grid_kernel(routes_any, owner_any, counts_any, query_any, scale_any, train, out,
+                routes, owner, counts, query, scale_tiles, scale, pairs_held,
+                mine, other, held, train_vmem, norm, picked, select, near_table, far_table,
+                results, collected, outgoing, incoming,
+                raw_sem, load_sem, z_send, z_recv, y_send, y_recv, c_send, c_recv, s_send, s_recv):
     rows, features = query.shape
+    fan = routes.shape[0]
+    half = features // 2
     pair = 2 * rows
     total = held.shape[2]
     extra = total - pair
@@ -86,12 +90,15 @@
     across = place * 4 + (1 - side) * 2 + core
     after, before = me + 4, me - 4
 
+    loads = [pltpu.make_async_copy(source, target, load_sem.at[i]) for i, (source, target) in enumerate(
+        [(query_any, query), (scale_any, scale_tiles), (routes_any, routes),
+         (owner_any, owner), (counts_any, counts), (train, train_vmem)])]
+    for load in loads:
+        load.start()
     barrier = pltpu.get_barrier_semaphore()
     for hop in range(1, shards):
         pl.semaphore_signal(barrier, inc=1, device_id={"train": (me + hop) % shards},
                             device_id_type=pl.DeviceIdType.MESH)
-    load = pltpu.make_async_copy(train, train_vmem, train_sem)
-    load.start()
 
     def remote(source, target, send, recv, device):
         return pltpu.make_async_remote_copy(
@@ -119,16 +126,37 @@
         order = jnp.dot(jnp.broadcast_to(hit, (8, pair)), earlier, preferred_element_type=jnp.float32)[:1]
         return hit, order.astype(jnp.int32)
 
-    def spread(block):
-        def body(i, total_square):
-            at = pl.ds(pl.multiple_of(i * width, width), width)
-            value = block[:, at].astype(jnp.float32) * scale[:, at]
-            return total_square + jnp.sum(value * value, axis=1, keepdims=True)
-        square = lax.fori_loop(0, features // width, body, jnp.zeros((rows, 1), jnp.float32))
-        return jnp.sqrt(square / features + 1e-06)
-
+    for load in loads[:2]:
+        load.wait()
+    for i in range(features // 128):
+        scale[:, pl.ds(i * 128, 128)] = scale_tiles[i:i + 1, :]
+
+    def squares(i, total_square):
+        at = pl.ds(pl.multiple_of(i * width, width), width)
+        value = query[:, at].astype(jnp.float32) * scale[:, at]
+        return total_square + jnp.sum(value * value, axis=1, keepdims=True)
+
+    square = lax.fori_loop(0, 2 * PARTS, squares, jnp.zeros((rows, 1), jnp.float32))
+    spread = jnp.sqrt(square / features + 1e-06)
+
+    def normalize_part(part, carry):
+        for lane in range(2):
+            at = pl.ds(pl.multiple_of(lane * half + part * width, width), width)
+            value = query[:, at].astype(jnp.float32) * scale[:, at]
+            mine[lane, part] = (value / spread).astype(jnp.bfloat16)
+        return carry
+
+    lax.fori_loop(0, PARTS, normalize_part, 0)
+    pl.semaphore_wait(barrier, shards - 1)
+    swap = remote(mine.at[1 - core], other, raw_sem.at[0], raw_sem.at[1], mate)
+    swap.start()
+
+    for load in loads[2:5]:
+        load.wait()
+    for i in range(2 * LINE):
+        pairs_held[i] = routes[:, i * pair:(i + 1) * pair]
     for origin in range(LINE):
-        pairs = routes_pairs[origin * 2 + side]
+        pairs = pairs_held[origin * 2 + side]
         tables = []
         for core_there in range(2):
             hit, order = slots(pairs, place * 4 + (1 - side) * 2 + core_there)
@@ -140,15 +168,7 @@
         order = jnp.where(second_core, tables[1][1], tables[0][1])
         chosen = (hit > 0.5) & (order == line % CAP) & (line // (2 * CAP) == lane // rows)
         select[origin] = chosen.astype(jnp.float32).astype(jnp.bfloat16)
-
-    my_spread = spread(query)
-    pl.semaphore_wait(barrier, shards - 1)
-    swap = remote(query, other, raw_sem.at[0], raw_sem.at[1], mate)
-    swap.start()
     swap.wait_recv()
-    their_spread = spread(other)
-    spread_first = jnp.where(core == 0, my_spread, their_spread)
-    spread_second = jnp.where(core == 0, their_spread, my_spread)
 
     def cross(origin, part):
         block = held[origin, core * PARTS + part, pl.ds(0, pair), :]
@@ -157,11 +177,10 @@
         y_copy(origin, part).start()
 
     def first(part, carry):
-        at = pl.ds(pl.multiple_of((core * PARTS + part) * width, width), width)
-        mine = query[:, at].astype(jnp.float32) * scale[:, at]
-        theirs = other[:, at].astype(jnp.float32) * scale[:, at]
-        top = jnp.where(core == 0, mine, theirs) / spread_first
-        low = jnp.where(core == 0, theirs, mine) / spread_second
+        ours = mine[core, part].astype(jnp.float32)
+        theirs = other[part].astype(jnp.float32)
+        top = jnp.where(core == 0, ours, theirs)
+        low = jnp.where(core == 0, theirs, ours)
         held[place, core * PARTS + part, pl.ds(0, pair), :] = jnp.concatenate([top, low], axis=0).astype(jnp.bfloat16)
 
         @pl.when(place < LINE - 1)
@@ -234,62 +253,86 @@
             return carry
         lax.fori_loop(0, PARTS, body, 0)
 
+    def collect(step):
+        for condition, origin, _ in sources(step):
+            def body(origin=origin):
+                collected[...] += jnp.dot(
+                    near_table[origin], results[origin, pl.ds(0, pair), :],
+                    precision=lax.Precision.HIGHEST, preferred_element_type=jnp.float32)
+                collected[...] += jnp.dot(
+                    far_table[origin], results[origin, pl.ds(pair, extra), :],
+                    precision=lax.Precision.HIGHEST, preferred_element_type=jnp.float32)
+            under(condition, body)
+
     results[...] = jnp.zeros_like(results)
-    load.wait()
-
-    def square(i, sums):
-        at = pl.ds(pl.multiple_of(i * 128, 128), 128)
-        value = train_vmem[:, at].astype(jnp.float32)
-        return sums + value * value
-
-    sums = lax.fori_loop(0, features // 128, square, jnp.zeros((columns, 128), jnp.float32))
-    sums = jnp.sum(jnp.transpose(sums), axis=0, keepdims=True)
-    norm = jnp.sqrt(sums / features + 1e-06) * math.sqrt(features)
-    live = lax.broadcasted_iota(jnp.int32, (1, columns), 1) < counts[0]
-    scaled[...] = norm
-
-    loop((arrive, 1), (crossed, 0))
-    loop((multiply, 0))
-    loop((arrive, 2), (crossed, 1))
-    loop((multiply, 1))
-
-    flat = jnp.zeros((1, routes_flat.shape[1]), jnp.int32)
-    for block in range(shards):
-        flat = flat + jnp.where(owner[block] == me, routes_flat[block:block + 1, :], 0)
-    lanes = flat.shape[1]
-    fan = routes_pairs.shape[1]
-    wide = jnp.broadcast_to(flat.astype(jnp.float32), (lanes, lanes))
-    same = jnp.transpose(wide) == wide
-    first_lane = lax.broadcasted_iota(jnp.int32, (lanes, lanes), 0) // fan
-    second_lane = lax.broadcasted_iota(jnp.int32, (lanes, lanes), 1) // fan
-    order = jnp.sum((same & (first_lane < second_lane)).astype(jnp.int32), axis=0, keepdims=True)
-    goal = flat * CAP + order
-    pickup = (lax.broadcasted_iota(jnp.int32, (shards * CAP, lanes), 0) == goal).astype(jnp.float32)
-    pickup = jnp.transpose(pickup)
-
-    loop((arrive, 3), (crossed, 2))
-    loop((multiply, 2))
-    loop((crossed, 3), (multiply, 3))
-
-    gathered = jnp.zeros((shards * CAP, columns), jnp.float32)
+    collected[...] = jnp.zeros_like(collected)
+
     for origin in range(LINE):
-        hit, order = slots(routes_pairs[origin * 2 + side], me)
+        hit, order = slots(pairs_held[origin * 2 + side], me)
         line = lax.broadcasted_iota(jnp.int32, (shards * CAP, pair), 0)
         lane = lax.broadcasted_iota(jnp.int32, (shards * CAP, pair), 1)
         near = (origin * 2 + side) * 2
         home = jnp.where(lane < rows, owner[near], owner[near + 1])
-        chosen = ((hit > 0.5) & (order == line % CAP) & (home == line // CAP)).astype(jnp.float32)
-        gathered = gathered + jnp.dot(chosen, results[origin, :pair], precision=lax.Precision.HIGHEST,
-                                      preferred_element_type=jnp.float32)
+        chosen = (hit > 0.5) & (order == line % CAP) & (home == line // CAP)
+        near_table[origin] = chosen.astype(jnp.float32)
         line = lax.broadcasted_iota(jnp.int32, (shards * CAP, extra), 0)
         lane = lax.broadcasted_iota(jnp.int32, (shards * CAP, extra), 1)
         far = (origin * 2 + 1 - side) * 2
         home = jnp.where(lane < 2 * CAP, owner[far], owner[far + 1])
         chosen = ((lane // CAP) % 2 == core) & (lane % CAP == line % CAP) & (home == line // CAP)
-        gathered = gathered + jnp.dot(chosen.astype(jnp.float32), results[origin, pair:],
-                                      precision=lax.Precision.HIGHEST, preferred_element_type=jnp.float32)
-    gathered = jnp.where(live, gathered / scaled[...], 0.0)
-    outgoing[...] = gathered.reshape(shards, CAP, columns)
+        far_table[origin] = chosen.astype(jnp.float32)
+
+    loop((arrive, 1), (crossed, 0))
+    loads[5].wait()
+
+    def train_squares(i, sums):
+        at = pl.ds(pl.multiple_of(i * 512, 512), 512)
+        value = train_vmem[:, at].astype(jnp.float32)
+        value = value * value
+        return sums + (value[:, :128] + value[:, 128:256]) + (value[:, 256:384] + value[:, 384:])
+
+    sums = lax.fori_loop(0, features // 512, train_squares, jnp.zeros((columns, 128), jnp.float32))
+    sums = jnp.sum(jnp.transpose(sums), axis=0, keepdims=True)
+    norm[...] = jnp.sqrt(sums / features + 1e-06) * math.sqrt(features)
+    loop((multiply, 0))
+    collect(0)
+    loop((arrive, 2), (crossed, 1))
+    loop((multiply, 1))
+    collect(1)
+
+    table = jnp.zeros((fan, rows), jnp.int32)
+    for block in range(shards):
+        table = table + jnp.where(owner[block] == me, routes[:, block * rows:(block + 1) * rows], 0)
+    lanes = rows * fan
+    flat = jnp.concatenate([table[j:j + 1] for j in range(fan)], axis=1)
+    wide = jnp.broadcast_to(flat.astype(jnp.float32), (lanes, lanes))
+    first_lane = lax.broadcasted_iota(jnp.int32, (lanes, lanes), 0)
+    second_lane = lax.broadcasted_iota(jnp.int32, (lanes, lanes), 1)
+    earlier = (jnp.transpose(wide) == wide) & (first_lane % rows < second_lane % rows)
+    goal = flat * CAP + jnp.sum(earlier.astype(jnp.int32), axis=0, keepdims=True)
+    moved = ((first_lane // rows == second_lane % fan) & (first_lane % rows == second_lane // fan)).astype(jnp.float32)
+    goal = jnp.dot(jnp.broadcast_to(goal.astype(jnp.float32), (8, lanes)), moved,
+                   precision=lax.Precision.HIGHEST, preferred_element_type=jnp.float32)[:1].astype(jnp.int32)
+    pickup = (lax.broadcasted_iota(jnp.int32, (shards * CAP, lanes), 0) == goal).astype(jnp.float32)
+    pickup = jnp.transpose(pickup)
+
+    def second_last(part, carry):
+        crossed(2, part)
+        multiply(2, part)
+        return carry
+
+    def last(turn, carry):
+        pl.when(turn < PARTS)(lambda: arrive(3, turn))
+        pl.when((turn >= 1) & (turn <= PARTS))(lambda: crossed(3, turn - 1))
+        pl.when(turn >= 2)(lambda: multiply(3, turn - 2))
+        return carry
+
+    lax.fori_loop(0, PARTS, second_last, 0)
+    collect(2)
+    lax.fori_loop(0, PARTS + 2, last, 0)
+    collect(3)
+    live = lax.broadcasted_iota(jnp.int32, (1, columns), 1) < counts[0]
+    outgoing[...] = jnp.where(live, collected[...] / norm[...], 0.0).reshape(shards, CAP, columns)
     incoming[me] = outgoing[me]
 
     def score_copy(hop, peer):
@@ -343,28 +386,37 @@
     shards = 4 * LINE
     pair, extra = 2 * rows, 4 * CAP
     width = features // (2 * PARTS)
-    routes_pairs = jnp.transpose(routes.reshape(2 * LINE, pair, fan), (0, 2, 1))
-    routes_flat = routes.reshape(shards, rows * fan)
     vmem = pl.BlockSpec(memory_space=pltpu.VMEM)
-    smem = pl.BlockSpec(memory_space=pltpu.SMEM)
+    left = pl.BlockSpec(memory_space=pltpu.HBM)
     dma = pltpu.SemaphoreType.DMA
     out = pl.pallas_call(
         grid_kernel,
         out_shape=jax.ShapeDtypeStruct((rows * fan, columns), jnp.float32),
-        in_specs=[vmem, vmem, smem, smem, vmem, vmem, pl.BlockSpec(memory_space=pl.ANY)],
+        in_specs=[left] * 6,
         out_specs=vmem,
         scratch_shapes=[
+            pltpu.VMEM(routes.shape[::-1], jnp.int32),
+            pltpu.SMEM(owner.shape, jnp.int32),
+            pltpu.SMEM(counts.shape, jnp.int32),
             pltpu.VMEM((rows, features), jnp.bfloat16),
+            pltpu.VMEM((features // 128, 128), jnp.float32),
+            pltpu.VMEM((1, features), jnp.float32),
+            pltpu.VMEM((2 * LINE, fan, pair), jnp.int32),
+            pltpu.VMEM((2, PARTS, rows, width), jnp.bfloat16),
+            pltpu.VMEM((PARTS, rows, width), jnp.bfloat16),
             pltpu.VMEM((LINE, 2 * PARTS, pair + extra, width), jnp.bfloat16),
             pltpu.VMEM((columns, features), jnp.bfloat16),
             pltpu.VMEM((1, columns), jnp.float32),
             pltpu.VMEM((LINE, PARTS, extra, width), jnp.bfloat16),
             pltpu.VMEM((LINE, extra, pair), jnp.bfloat16),
+            pltpu.VMEM((LINE, shards * CAP, pair), jnp.float32),
+            pltpu.VMEM((LINE, shards * CAP, extra), jnp.float32),
             pltpu.VMEM((LINE, pair + extra, columns), jnp.float32),
+            pltpu.VMEM((shards * CAP, columns), jnp.float32),
             pltpu.VMEM((shards, CAP, columns), jnp.float32),
             pltpu.VMEM((shards, CAP, columns), jnp.float32),
             dma((2,)),
-            dma,
+            dma((6,)),
             dma((2, LINE - 1, PARTS)),
             dma((LINE, PARTS)),
             dma((LINE, PARTS)),
@@ -375,8 +427,8 @@
             dma((shards,)),
         ],
         compiler_params=pltpu.CompilerParams(
-            collective_id=0, has_side_effects=True, vmem_limit_bytes=40 * 1024 * 1024),
-    )(routes_pairs, routes_flat, owner, counts, query_grads, precondition.reshape(1, features), train_grads)
+            collective_id=0, has_side_effects=True, vmem_limit_bytes=63 * 1024 * 1024),
+    )(routes.T, owner, counts, query_grads, precondition.reshape(features // 128, 128), train_grads)
     return out.reshape(rows, fan, columns)
 
 

time: 58.9 us -> 54.5 us (0.925)
  local copies, waits for them, and re-layouts: 6.97 us -> 1.56 us
  Pallas kernels: 50.9 us -> 52.1 us
    unnamed x9 -> x0, local copies, waits for them, and re-layouts: 5.41 us -> none
    pallas_call x1, Pallas kernels: 50.9 us -> 52.1 us  [on_grid(): pl.pallas_call(grid_kernel, out_shape=jax.ShapeDtypeStruct((rows * fan, c...]
    reshape x1, local copies, waits for them, and re-layouts: 0.67 us -> 1.56 us  [on_grid(): return out.reshape(rows, fan, columns)]
    reshape x3 -> x0, local copies, waits for them, and re-layouts: 0.89 us -> none  [the longest x2 0.78 us: on_grid(): routes_pairs = jnp.transpose(routes.reshape(2 * LINE, pair, fan), (0, 2, 1))]
where the time goes in v2:
time: 54.5 us; the launch traced here: 54.3 us
  Pallas kernels  52.1 us (96%)
  local copies, waits for them, and re-layouts  1.56 us (3%)
  between operations  0.66 us (1%)
    pallas_call x1, Pallas kernels, on_grid(): pl.pallas_call(grid_kernel, out_shape=jax.ShapeDtypeStruct((rows * fan, c...  52.1 us
    reshape x1, local copies, waits for them, and re-layouts, on_grid(): return out.reshape(rows, fan, columns)  1.56 us

profile of v2, /device:TPU:0, one launch (start us, length us, event | category | flops | bytes accessed | tf_op | source)
XLA Modules:
  0.0 54.3 jit_solution(10427971477317825200)
XLA Ops:
  0.7 52.1 %shard_map.64 = f32[96,256]{1,0:T(8,128)} custom-call(s32[4,384]{1,0:T(4,128)} %bitcast.3, s32[16]{0:T(128)} %owner_any.1, s32[1]{0:T(128)S(6)} %copy.7.counts_any, bf16[24,8192]{1,0:T(8,128)(2,1)} %query_any.1, f32[64,128]{1,0:T(8,128)} %bitcast.2, bf16[256,8192]{1,0:T(8,128)(2,1)} %train.1), custom_call_target="tpu_custom_call" | custom-call | tf_op jit(solution)/shard_map/pallas_call | solution.py:392
  52.7 1.6 %reshape.7 = f32[24,4,256]{2,1,0:T(4,128)} reshape(f32[96,256]{1,0:T(8,128)} %shard_map.64) | data formatting | bytes 196608 | tf_op jit(solution)/shard_map/reshape | solution.py:432

commit v3 on v2

--- a/solution.py
+++ b/solution.py
@@ -65,12 +65,12 @@
 
 
 LINE = 4
-PARTS = 4
+PARTS = 2
 
 
 def grid_kernel(routes_any, owner_any, counts_any, query_any, scale_any, train, out,
                 routes, owner, counts, query, scale_tiles, scale, pairs_held,
-                mine, other, held, train_vmem, norm, picked, select, near_table, far_table,
+                mine, other, held, train_vmem, norm, picked, select, table,
                 results, collected, outgoing, incoming,
                 raw_sem, load_sem, z_send, z_recv, y_send, y_recv, c_send, c_recv, s_send, s_recv):
     rows, features = query.shape
@@ -118,14 +118,6 @@
         block = held.at[origin, lane * PARTS + part, span]
         return remote(block, block, c_send.at[kind, origin, part], c_recv.at[kind, origin, part], mate)
 
-    def slots(pairs, shard):
-        hit = jnp.sum((pairs == shard).astype(jnp.float32), axis=0, keepdims=True)
-        first = lax.broadcasted_iota(jnp.int32, (pair, pair), 0)
-        second = lax.broadcasted_iota(jnp.int32, (pair, pair), 1)
-        earlier = ((first // rows == second // rows) & (first < second)).astype(jnp.float32)
-        order = jnp.dot(jnp.broadcast_to(hit, (8, pair)), earlier, preferred_element_type=jnp.float32)[:1]
-        return hit, order.astype(jnp.int32)
-
     for load in loads[:2]:
         load.wait()
     for i in range(features // 128):
@@ -155,18 +147,27 @@
         load.wait()
     for i in range(2 * LINE):
         pairs_held[i] = routes[:, i * pair:(i + 1) * pair]
+    lane = lax.broadcasted_iota(jnp.int32, (1, pair), 1)
+    second_block = lane >= rows
+    targets = [place * 4 + (1 - side) * 2, place * 4 + (1 - side) * 2 + 1, me]
+    hits = []
     for origin in range(LINE):
         pairs = pairs_held[origin * 2 + side]
-        tables = []
+        for shard in targets:
+            hits.append(jnp.sum((pairs == shard).astype(jnp.float32), axis=0, keepdims=True))
+    hits = jnp.concatenate(hits + hits[:4], axis=0)
+    first_lane = lax.broadcasted_iota(jnp.int32, (pair, pair), 0)
+    second_lane = lax.broadcasted_iota(jnp.int32, (pair, pair), 1)
+    earlier = ((first_lane < rows) == (second_lane < rows)) & (first_lane < second_lane)
+    orders = jnp.dot(hits, earlier.astype(jnp.float32), preferred_element_type=jnp.float32).astype(jnp.int32)
+    line = lax.broadcasted_iota(jnp.int32, (extra, pair), 0)
+    for origin in range(LINE):
+        chosen = None
         for core_there in range(2):
-            hit, order = slots(pairs, place * 4 + (1 - side) * 2 + core_there)
-            tables.append((hit, order))
-        line = lax.broadcasted_iota(jnp.int32, (extra, pair), 0)
-        lane = lax.broadcasted_iota(jnp.int32, (extra, pair), 1)
-        second_core = (line // CAP) % 2 == 1
-        hit = jnp.where(second_core, tables[1][0], tables[0][0])
-        order = jnp.where(second_core, tables[1][1], tables[0][1])
-        chosen = (hit > 0.5) & (order == line % CAP) & (line // (2 * CAP) == lane // rows)
+            at = origin * 3 + core_there
+            goal = jnp.where(second_block, 2 * CAP, 0) + core_there * CAP + orders[at:at + 1]
+            same = line == jnp.where(hits[at:at + 1] > 0.5, goal, -1)
+            chosen = same if chosen is None else chosen | same
         select[origin] = chosen.astype(jnp.float32).astype(jnp.bfloat16)
     swap.wait_recv()
 
@@ -257,30 +258,27 @@
         for condition, origin, _ in sources(step):
             def body(origin=origin):
                 collected[...] += jnp.dot(
-                    near_table[origin], results[origin, pl.ds(0, pair), :],
-                    precision=lax.Precision.HIGHEST, preferred_element_type=jnp.float32)
-                collected[...] += jnp.dot(
-                    far_table[origin], results[origin, pl.ds(pair, extra), :],
+                    table[origin], results[origin],
                     precision=lax.Precision.HIGHEST, preferred_element_type=jnp.float32)
             under(condition, body)
 
     results[...] = jnp.zeros_like(results)
     collected[...] = jnp.zeros_like(collected)
 
+    far_lane = lax.broadcasted_iota(jnp.int32, (1, extra), 1)
+    far_second = far_lane >= 2 * CAP
+    far_slot = far_lane - jnp.where(far_second, 2 * CAP, 0) - core * CAP
+    far_valid = (far_slot >= 0) & (far_slot < CAP)
+    tall = lax.broadcasted_iota(jnp.int32, (shards * CAP, total), 0)
     for origin in range(LINE):
-        hit, order = slots(pairs_held[origin * 2 + side], me)
-        line = lax.broadcasted_iota(jnp.int32, (shards * CAP, pair), 0)
-        lane = lax.broadcasted_iota(jnp.int32, (shards * CAP, pair), 1)
+        at = origin * 3 + 2
         near = (origin * 2 + side) * 2
-        home = jnp.where(lane < rows, owner[near], owner[near + 1])
-        chosen = (hit > 0.5) & (order == line % CAP) & (home == line // CAP)
-        near_table[origin] = chosen.astype(jnp.float32)
-        line = lax.broadcasted_iota(jnp.int32, (shards * CAP, extra), 0)
-        lane = lax.broadcasted_iota(jnp.int32, (shards * CAP, extra), 1)
+        home = jnp.where(second_block, owner[near + 1], owner[near])
+        near_goal = jnp.where(hits[at:at + 1] > 0.5, home * CAP + orders[at:at + 1], -1)
         far = (origin * 2 + 1 - side) * 2
-        home = jnp.where(lane < 2 * CAP, owner[far], owner[far + 1])
-        chosen = ((lane // CAP) % 2 == core) & (lane % CAP == line % CAP) & (home == line // CAP)
-        far_table[origin] = chosen.astype(jnp.float32)
+        home = jnp.where(far_second, owner[far + 1], owner[far])
+        far_goal = jnp.where(far_valid, home * CAP + far_slot, -1)
+        table[origin] = (tall == jnp.concatenate([near_goal, far_goal], axis=1)).astype(jnp.float32)
 
     loop((arrive, 1), (crossed, 0))
     loads[5].wait()
@@ -295,41 +293,41 @@
     sums = jnp.sum(jnp.transpose(sums), axis=0, keepdims=True)
     norm[...] = jnp.sqrt(sums / features + 1e-06) * math.sqrt(features)
     loop((multiply, 0))
+    arrive(2, 0)
+    crossed(1, 0)
     collect(0)
-    loop((arrive, 2), (crossed, 1))
-    loop((multiply, 1))
+    multiply(1, 0)
+    arrive(2, 1)
+    crossed(1, 1)
+    multiply(1, 1)
     collect(1)
 
-    table = jnp.zeros((fan, rows), jnp.int32)
+    named = jnp.zeros((fan, rows), jnp.int32)
     for block in range(shards):
-        table = table + jnp.where(owner[block] == me, routes[:, block * rows:(block + 1) * rows], 0)
+        named = named + jnp.where(owner[block] == me, routes[:, block * rows:(block + 1) * rows], 0)
     lanes = rows * fan
-    flat = jnp.concatenate([table[j:j + 1] for j in range(fan)], axis=1)
+    flat = jnp.concatenate([named[j:j + 1] for j in range(fan)], axis=1)
     wide = jnp.broadcast_to(flat.astype(jnp.float32), (lanes, lanes))
     first_lane = lax.broadcasted_iota(jnp.int32, (lanes, lanes), 0)
     second_lane = lax.broadcasted_iota(jnp.int32, (lanes, lanes), 1)
-    earlier = (jnp.transpose(wide) == wide) & (first_lane % rows < second_lane % rows)
+    first_query = first_lane - rows * sum((first_lane >= rows * j).astype(jnp.int32) for j in range(1, fan))
+    second_query = second_lane - rows * sum((second_lane >= rows * j).astype(jnp.int32) for j in range(1, fan))
+    earlier = (jnp.transpose(wide) == wide) & (first_query < second_query)
     goal = flat * CAP + jnp.sum(earlier.astype(jnp.int32), axis=0, keepdims=True)
-    moved = ((first_lane // rows == second_lane % fan) & (first_lane % rows == second_lane // fan)).astype(jnp.float32)
+    moved = ((first_lane - first_query) + first_query * (rows * fan) == (second_lane % fan) * rows + (second_lane // fan) * (rows * fan)).astype(jnp.float32)
     goal = jnp.dot(jnp.broadcast_to(goal.astype(jnp.float32), (8, lanes)), moved,
                    precision=lax.Precision.HIGHEST, preferred_element_type=jnp.float32)[:1].astype(jnp.int32)
     pickup = (lax.broadcasted_iota(jnp.int32, (shards * CAP, lanes), 0) == goal).astype(jnp.float32)
     pickup = jnp.transpose(pickup)
 
-    def second_last(part, carry):
-        crossed(2, part)
-        multiply(2, part)
-        return carry
-
-    def last(turn, carry):
-        pl.when(turn < PARTS)(lambda: arrive(3, turn))
-        pl.when((turn >= 1) & (turn <= PARTS))(lambda: crossed(3, turn - 1))
-        pl.when(turn >= 2)(lambda: multiply(3, turn - 2))
-        return carry
-
-    lax.fori_loop(0, PARTS, second_last, 0)
+    arrive(3, 0)
+    loop((crossed, 2), (multiply, 2))
     collect(2)
-    lax.fori_loop(0, PARTS + 2, last, 0)
+    crossed(3, 0)
+    arrive(3, 1)
+    multiply(3, 0)
+    crossed(3, 1)
+    multiply(3, 1)
     collect(3)
     live = lax.broadcasted_iota(jnp.int32, (1, columns), 1) < counts[0]
     outgoing[...] = jnp.where(live, collected[...] / norm[...], 0.0).reshape(shards, CAP, columns)
@@ -409,8 +407,7 @@
             pltpu.VMEM((1, columns), jnp.float32),
             pltpu.VMEM((LINE, PARTS, extra, width), jnp.bfloat16),
             pltpu.VMEM((LINE, extra, pair), jnp.bfloat16),
-            pltpu.VMEM((LINE, shards * CAP, pair), jnp.float32),
-            pltpu.VMEM((LINE, shards * CAP, extra), jnp.float32),
+            pltpu.VMEM((LINE, shards * CAP, pair + extra), jnp.float32),
             pltpu.VMEM((LINE, pair + extra, columns), jnp.float32),
             pltpu.VMEM((shards * CAP, columns), jnp.float32),
             pltpu.VMEM((shards, CAP, columns), jnp.float32),

time: 54.5 us -> 49.4 us (0.906)
  Pallas kernels: 52.1 us -> 47.1 us
    pallas_call x1, Pallas kernels: 52.1 us -> 47.1 us  [on_grid(): pl.pallas_call(grid_kernel, out_shape=jax.ShapeDtypeStruct((rows * fan, c...]
where the time goes in v3:
time: 49.4 us; the launch traced here: 49.3 us
  Pallas kernels  47.1 us (95%)
  local copies, waits for them, and re-layouts  1.56 us (3%)
  between operations  0.66 us (1%)
    pallas_call x1, Pallas kernels, on_grid(): pl.pallas_call(grid_kernel, out_shape=jax.ShapeDtypeStruct((rows * fan, c...  47.1 us
    reshape x1, local copies, waits for them, and re-layouts, on_grid(): return out.reshape(rows, fan, columns)  1.56 us

profile of v3, /device:TPU:0, one launch (start us, length us, event | category | flops | bytes accessed | tf_op | source)
XLA Modules:
  0.0 49.3 jit_solution(4129344235623956503)
XLA Ops:
  0.7 47.1 %shard_map.64 = f32[96,256]{1,0:T(8,128)} custom-call(s32[4,384]{1,0:T(4,128)} %bitcast.3, s32[16]{0:T(128)} %owner_any.1, s32[1]{0:T(128)S(6)} %copy.7.counts_any, bf16[24,8192]{1,0:T(8,128)(2,1)} %query_any.1, f32[64,128]{1,0:T(8,128)} %bitcast.2, bf16[256,8192]{1,0:T(8,128)(2,1)} %train.1), custom_call_target="tpu_custom_call" | custom-call | tf_op jit(solution)/shard_map/pallas_call | solution.py:390
  47.7 1.6 %reshape.7 = f32[24,4,256]{2,1,0:T(4,128)} reshape(f32[96,256]{1,0:T(8,128)} %shard_map.64) | data formatting | bytes 196608 | tf_op jit(solution)/shard_map/reshape | solution.py:429

commit v4 on v3

--- a/solution.py
+++ b/solution.py
@@ -129,13 +129,13 @@
         return total_square + jnp.sum(value * value, axis=1, keepdims=True)
 
     square = lax.fori_loop(0, 2 * PARTS, squares, jnp.zeros((rows, 1), jnp.float32))
-    spread = jnp.sqrt(square / features + 1e-06)
+    spread = 1.0 / jnp.sqrt(square / features + 1e-06)
 
     def normalize_part(part, carry):
         for lane in range(2):
             at = pl.ds(pl.multiple_of(lane * half + part * width, width), width)
             value = query[:, at].astype(jnp.float32) * scale[:, at]
-            mine[lane, part] = (value / spread).astype(jnp.bfloat16)
+            mine[lane, part] = (value * spread).astype(jnp.bfloat16)
         return carry
 
     lax.fori_loop(0, PARTS, normalize_part, 0)
@@ -193,10 +193,11 @@
             z_copy(1, 0, place, part, before).start()
 
         c_copy(0, place, part, core).start()
+        return carry
+
+    lax.fori_loop(0, PARTS, first, 0)
+    for part in range(PARTS):
         cross(place, part)
-        return carry
-
-    lax.fori_loop(0, PARTS, first, 0)
 
     def sources(step):
         if step == 0:
@@ -223,6 +224,9 @@
                         def _():
                             z_copy(1, step, origin, part, before).start()
                 c_copy(0, origin, part, core).start()
+            under(condition, body)
+        for condition, origin, direction in sources(step):
+            def body(origin=origin):
                 cross(origin, part)
             under(condition, body)
 

time: 49.4 us -> 49.4 us (level)
  no operation moved by 1% of the time
where the time goes in v4:
time: 49.4 us; the launch traced here: 49.3 us
  Pallas kernels  47.1 us (95%)
  local copies, waits for them, and re-layouts  1.56 us (3%)
  between operations  0.66 us (1%)
    pallas_call x1, Pallas kernels, on_grid(): pl.pallas_call(grid_kernel, out_shape=jax.ShapeDtypeStruct((rows * fan, c...  47.1 us
    reshape x1, local copies, waits for them, and re-layouts, on_grid(): return out.reshape(rows, fan, columns)  1.56 us

profile of v4, /device:TPU:0, one launch (start us, length us, event | category | flops | bytes accessed | tf_op | source)
XLA Modules:
  0.0 49.3 jit_solution(6509144945680918606)
XLA Ops:
  0.7 47.1 %shard_map.64 = f32[96,256]{1,0:T(8,128)} custom-call(s32[4,384]{1,0:T(4,128)} %bitcast.3, s32[16]{0:T(128)} %owner_any.1, s32[1]{0:T(128)S(6)} %copy.7.counts_any, bf16[24,8192]{1,0:T(8,128)(2,1)} %query_any.1, f32[64,128]{1,0:T(8,128)} %bitcast.2, bf16[256,8192]{1,0:T(8,128)(2,1)} %train.1), custom_call_target="tpu_custom_call" | custom-call | tf_op jit(solution)/shard_map/pallas_call | solution.py:394
  47.7 1.6 %reshape.7 = f32[24,4,256]{2,1,0:T(4,128)} reshape(f32[96,256]{1,0:T(8,128)} %shard_map.64) | data formatting | bytes 196608 | tf_op jit(solution)/shard_map/reshape | solution.py:433
